TPU v7x, 1024 devices: a whole 8x8x8 slice. The times are simulated.
1024 devices in a mesh: edata: 8 (over z), node: 16 (over x, core), local: 8 (over y).
Axes of the slice: x: 8, y: 8, z: 8, core: 2. Of those that a mesh axis runs over, the one named last changes fastest.
Arguments:
- tokens: bfloat16 [8192, 2048], P(('edata', 'node', 'local')), may hold values from -6 to 6
- cotangent: bfloat16 [8192, 2048], P(('edata', 'node', 'local')), may hold values from -6 to 6
- expert_ids: int32 [8192, 8], P(('edata', 'node', 'local')), may hold values from 0 to 127, as said below
- route_weights: bfloat16 [8192, 8], P(('edata', 'node', 'local')), may hold values from 0.049804688 to 0.5
- w_gate: bfloat16 [128, 2048, 768], P(('node', 'local')), may hold values from -0.125 to 0.125
- w_up: bfloat16 [128, 2048, 768], P(('node', 'local')), may hold values from -0.125 to 0.125
- w_down: bfloat16 [128, 768, 2048], P(('node', 'local')), may hold values from -0.21875 to 0.21875
Outputs:
- token_grad: bfloat16 [8192, 2048], P(('edata', 'node', 'local'))
- weight_grad: bfloat16 [8192, 8], P(('edata', 'node', 'local'))
- down_grad: float32 [128, 768, 2048], P(('node', 'local'), 'edata')
Inputs may be any that keep to these rules, and one draw needn't show every extreme that they name: `expert_ids`: each row names 8 different experts. Within the 128 tokens of the devices that share their edata and local indices, every expert is named by 0 or exactly 16 tokens, and one expert is named by 16 tokens in every such set.
All inputs are finite; a program needn't handle non-finite values.
Results may differ from a plain program's by a relative error of at most 0.015.
Values may be sent and summed in bfloat16 or wider, within the bound.
A program may use at most 64 MiB of HBM per device.

v0:
```python
import jax
import jax.numpy as jnp
from jax import lax
from jax.sharding import PartitionSpec as P


def body(tokens, cotangent, expert_ids, route_weights, w_gate, w_up, w_down):
    node_count = lax.axis_size("node")
    local_count = lax.axis_size("local")
    expert_total = node_count * local_count
    tok_count, model_width = tokens.shape
    top_count = expert_ids.shape[1]
    column_rows = node_count * tok_count
    slot_count = min(column_rows, 2 * column_rows * top_count // expert_total)
    picked = expert_ids[:, :, None] == jnp.arange(expert_total, dtype=jnp.int32)[None, None, :]
    dense_weights = jnp.sum(
        jnp.where(picked, route_weights[:, :, None].astype(jnp.float32), 0.0), axis=1
    )
    by_node = dense_weights.reshape(tok_count, node_count, local_count).transpose(1, 0, 2)
    touched = jnp.any(by_node > 0.0, axis=2)[:, :, None]
    node_weights = by_node.astype(jnp.bfloat16)
    zero_value = jnp.zeros((), jnp.bfloat16)
    node_tokens = jnp.where(touched, tokens[None, :, :], zero_value)
    got_tokens, got_weights = (
        lax.all_to_all(node_tokens, "node", split_axis=0, concat_axis=0, tiled=True),
        lax.all_to_all(node_weights, "node", split_axis=0, concat_axis=0, tiled=True),
    )
    flat_weights = got_weights.reshape(column_rows, local_count)
    live_mask = flat_weights != zero_value
    slot_rank = jnp.cumsum(live_mask.astype(jnp.int32), axis=0) - 1
    selector = (
        slot_rank.T[:, None, :] == jnp.arange(slot_count, dtype=jnp.int32)[None, :, None]
    ) & live_mask.T[:, None, :]
    selector = selector.astype(jnp.bfloat16)

    def pick_slots(rows):
        flat_rows = rows.reshape(column_rows, model_width)
        return jnp.einsum(
            "lsq,qd->lsd", selector, flat_rows, preferred_element_type=jnp.float32
        ).astype(jnp.bfloat16)

    slot_weights = jnp.einsum(
        "lsq,ql->ls", selector, flat_weights, preferred_element_type=jnp.float32
    ).astype(jnp.bfloat16)
    exp_tokens, exp_weights = (
        lax.all_to_all(pick_slots(got_tokens), "local", split_axis=0, concat_axis=0, tiled=True),
        lax.all_to_all(slot_weights, "local", split_axis=0, concat_axis=0, tiled=True),
    )
    gate_weight = w_gate[0]
    up_weight = w_up[0]
    down_weight = w_down[0]
    rows_in = exp_tokens.reshape(-1, model_width)
    gate_value = jnp.dot(rows_in, gate_weight, preferred_element_type=jnp.float32)
    up_value = jnp.dot(rows_in, up_weight, preferred_element_type=jnp.float32)
    sigmoid_gate = jax.nn.sigmoid(gate_value)
    silu_gate = gate_value * sigmoid_gate
    hidden = (silu_gate * up_value).astype(jnp.bfloat16)
    output = jnp.dot(hidden, down_weight, preferred_element_type=jnp.float32)
    node_grads = jnp.where(touched, cotangent[None, :, :], zero_value)
    got_grads = lax.all_to_all(node_grads, "node", split_axis=0, concat_axis=0, tiled=True)
    exp_grads = lax.all_to_all(
        pick_slots(got_grads), "local", split_axis=0, concat_axis=0, tiled=True
    )
    grads_in = exp_grads.reshape(-1, model_width)
    weight_rows = exp_weights.reshape(-1).astype(jnp.float32)
    weight_slot = jnp.sum(grads_in.astype(jnp.float32) * output, axis=1).astype(jnp.bfloat16)
    out_grad = (weight_rows[:, None] * grads_in.astype(jnp.float32)).astype(jnp.bfloat16)
    hidden_grad = lax.dot_general(
        out_grad, down_weight, (((1,), (1,)), ((), ())), preferred_element_type=jnp.float32
    )
    gate_grad = (
        hidden_grad * up_value * sigmoid_gate * (1.0 + gate_value * (1.0 - sigmoid_gate))
    ).astype(jnp.bfloat16)
    up_grad = (hidden_grad * silu_gate).astype(jnp.bfloat16)
    row_grads = lax.dot_general(
        gate_grad, gate_weight, (((1,), (1,)), ((), ())), preferred_element_type=jnp.float32
    )
    row_grads = row_grads + lax.dot_general(
        up_grad, up_weight, (((1,), (1,)), ((), ())), preferred_element_type=jnp.float32
    )
    row_grads = row_grads.astype(jnp.bfloat16)
    back_rows, back_weights = (
        lax.all_to_all(
            row_grads.reshape(local_count, slot_count, model_width),
            "local",
            split_axis=0,
            concat_axis=0,
            tiled=True,
        ),
        lax.all_to_all(
            weight_slot.reshape(local_count, slot_count),
            "local",
            split_axis=0,
            concat_axis=0,
            tiled=True,
        ),
    )
    group_rows = jnp.einsum(
        "lsq,lsd->qd", selector, back_rows, preferred_element_type=jnp.float32
    ).astype(jnp.bfloat16)
    group_rows = group_rows.reshape(node_count, tok_count, model_width)
    group_weights = jnp.einsum(
        "lsq,ls->ql", selector, back_weights, preferred_element_type=jnp.float32
    ).astype(jnp.bfloat16)
    group_weights = group_weights.reshape(node_count, tok_count, local_count)
    home_rows, home_weights = (
        lax.all_to_all(group_rows, "node", split_axis=0, concat_axis=0, tiled=True),
        lax.all_to_all(group_weights, "node", split_axis=0, concat_axis=0, tiled=True),
    )
    token_grad = jnp.sum(home_rows.astype(jnp.float32), axis=0).astype(jnp.bfloat16)
    weight_full = (
        home_weights.transpose(1, 0, 2).reshape(tok_count, expert_total).astype(jnp.float32)
    )
    weight_grad = jnp.sum(jnp.where(picked, weight_full[:, None, :], 0.0), axis=2).astype(
        jnp.bfloat16
    )
    down_grad = lax.psum_scatter(
        lax.dot_general(
            hidden, out_grad, (((0,), (0,)), ((), ())), preferred_element_type=jnp.float32
        ).astype(jnp.bfloat16),
        "edata",
        scatter_dimension=0,
        tiled=True,
    ).astype(jnp.float32)
    return (token_grad, weight_grad, down_grad[None, :, :])


def solution(mesh):
    in_specs = (
        P(("edata", "node", "local"), None),
        P(("edata", "node", "local"), None),
        P(("edata", "node", "local"), None),
        P(("edata", "node", "local"), None),
        P(("node", "local"), None, None),
        P(("node", "local"), None, None),
        P(("node", "local"), None, None),
    )
    out_specs = (
        P(("edata", "node", "local"), None),
        P(("edata", "node", "local"), None),
        P(("node", "local"), "edata", None),
    )
    return jax.shard_map(body, mesh=mesh, in_specs=in_specs, out_specs=out_specs, check_vma=False)
```

profile of v0, /device:TPU:1, one launch (start us, length us, event | category | flops | bytes accessed | tf_op | source)
XLA Modules:
  0.0 219.9 jit_solution(1034764237815697145)
XLA Ops:
  9.6 17.4 %all-to-all-start = ((bf16[16,8,8]{2,1,0:T(8,128)(2,1)}), bf16[16,8,8]{2,1,0:T(8,128)(2,1)S(1)}, u32[]{:S(2)}, u32[]{:S(2)}) async-start(bf16[16,8,8]{2,1,0:T(8,128)(2,1)} %copy.39), calls=%async_computation | async-start | bytes 65536 | tf_op jit(solution)/shard_map/all_to_all | solution.py:26
  27.5 7.1 %all-to-all-done = bf16[16,8,8]{2,1,0:T(8,128)(2,1)S(1)} async-done(((bf16[16,8,8]{2,1,0:T(8,128)(2,1)}), bf16[16,8,8]{2,1,0:T(8,128)(2,1)S(1)}, u32[]{:S(2)}, u32[]{:S(2)}) %all-to-all-start) | async-done | bytes 2080 | tf_op jit(solution)/shard_map/all_to_all | solution.py:26
  35.8 3.3 %all-to-all-start.1 = ((bf16[8,1,16]{2,1,0:T(2,128)(2,1)}), bf16[8,1,16]{2,1,0:T(2,128)(2,1)S(1)}, u32[]{:S(2)}, u32[]{:S(2)}) async-start(bf16[8,1,16]{2,1,0:T(2,128)(2,1)} %copy.43), calls=%async_computation.1 | async-start | bytes 8192 | tf_op jit(solution)/shard_map/all_to_all | solution.py:47
  39.1 1.9 broadcast_select_fusion.1
  41.0 4.5 %all-to-all-done.1 = bf16[8,1,16]{2,1,0:T(2,128)(2,1)S(1)} async-done(((bf16[8,1,16]{2,1,0:T(2,128)(2,1)}), bf16[8,1,16]{2,1,0:T(2,128)(2,1)S(1)}, u32[]{:S(2)}, u32[]{:S(2)}) %all-to-all-start.1) | async-done | bytes 288 | tf_op jit(solution)/shard_map/all_to_all | solution.py:47
  45.5 22.9 %all_to_all.58 = bf16[16,8,2048]{2,1,0:T(8,128)(2,1)} all-to-all(bf16[16,8,2048]{2,1,0:T(8,128)(2,1)} %get-tuple-element.6), channel_id=1, replica_groups=mesh['edata'=8,'node'=16,'local'=8] {'node'}, dimensions={0} | all-to-all | bytes 1048576 | tf_op jit(solution)/shard_map/all_to_all | solution.py:25
  68.4 4.1 %all-to-all-start.2 = ((bf16[16,8,2048]{2,1,0:T(8,128)(2,1)}), bf16[16,8,2048]{2,1,0:T(8,128)(2,1)}, u32[]{:S(2)}, u32[]{:S(2)}) async-start(bf16[16,8,2048]{2,1,0:T(8,128)(2,1)} %get-tuple-element.5), calls=%async_computation.2 | async-start | bytes 1048576 | tf_op jit(solution)/shard_map/all_to_all | solution.py:60
  72.5 2.1 convolution_convert_fusion.1
  74.7 14.0 %all-to-all-done.2 = bf16[16,8,2048]{2,1,0:T(8,128)(2,1)} async-done(((bf16[16,8,2048]{2,1,0:T(8,128)(2,1)}), bf16[16,8,2048]{2,1,0:T(8,128)(2,1)}, u32[]{:S(2)}, u32[]{:S(2)}) %all-to-all-start.2) | async-done | bytes 524320 | tf_op jit(solution)/shard_map/all_to_all | solution.py:60
  88.7 4.2 %all-to-all-start.5 = ((bf16[8,16,2048]{2,1,0:T(8,128)(2,1)}), bf16[8,16,2048]{2,1,0:T(8,128)(2,1)}, u32[]{:S(2)}, u32[]{:S(2)}) async-start(bf16[8,16,2048]{2,1,0:T(8,128)(2,1)} %convolution_convert_fusion.1), calls=%async_computation.5 | async-start | bytes 1048576 | tf_op jit(solution)/shard_map/all_to_all | solution.py:46
  92.9 2.1 convolution_convert_fusion.2
  95.0 15.3 %all-to-all-done.5 = bf16[8,16,2048]{2,1,0:T(8,128)(2,1)} async-done(((bf16[8,16,2048]{2,1,0:T(8,128)(2,1)}), bf16[8,16,2048]{2,1,0:T(8,128)(2,1)}, u32[]{:S(2)}, u32[]{:S(2)}) %all-to-all-start.5) | async-done | bytes 524320 | tf_op jit(solution)/shard_map/all_to_all | solution.py:46
  110.3 4.2 %all-to-all-start.3 = ((bf16[8,16,2048]{2,1,0:T(8,128)(2,1)}), bf16[8,16,2048]{2,1,0:T(8,128)(2,1)}, u32[]{:S(2)}, u32[]{:S(2)}) async-start(bf16[8,16,2048]{2,1,0:T(8,128)(2,1)} %convolution_convert_fusion.2), calls=%async_computation.3 | async-start | bytes 1048576 | tf_op jit(solution)/shard_map/all_to_all | solution.py:61
  114.6 2.6 %fusion.2 = f32[128,768]{1,0:T(8,128)S(1)} fusion(bf16[128,2048]{1,0:T(8,128)(2,1)} %bitcast.16, bf16[1,2048,768]{2,1,0:T(8,128)(2,1)} %param.11), kind=kOutput, calls=%fused_computation.3 | convolution fusion | flops 402653184 | bytes 4063232 | tf_op jit(solution)/shard_map/dot_general | solution.py:53
  117.2 2.5 %multiply_convert_fusion.1 = (bf16[128,768]{1,0:T(8,128)(2,1)}, f32[128,768]{1,0:T(8,128)}) fusion(f32[128,768]{1,0:T(8,128)S(1)} %fusion.2, bf16[128,2048]{1,0:T(8,128)(2,1)} %bitcast.16, bf16[1,2048,768]{2,1,0:T(8,128)(2,1)S(1)} %copy-done), kind=kOutput, calls=%fused_computation.30 | convolution fusion | flops 403243008 | bytes 4653056 | tf_op jit(solution)/shard_map/dot_general | solution.py:54
  119.7 12.7 %all-to-all-done.3 = bf16[8,16,2048]{2,1,0:T(8,128)(2,1)} async-done(((bf16[8,16,2048]{2,1,0:T(8,128)(2,1)}), bf16[8,16,2048]{2,1,0:T(8,128)(2,1)}, u32[]{:S(2)}, u32[]{:S(2)}) %all-to-all-start.3) | async-done | bytes 524320 | tf_op jit(solution)/shard_map/all_to_all | solution.py:61
  132.4 1.2 fusion.26
  133.6 3.6 %convolution_convert_fusion = bf16[768,2048]{1,0:T(8,128)(2,1)} fusion(bf16[128,768]{1,0:T(8,128)(2,1)} %get-tuple-element.9, bf16[128,2048]{1,0:T(8,128)(2,1)S(1)} %fusion.26), kind=kOutput, calls=%fused_computation | convolution fusion | flops 404226048 | bytes 3866624 | tf_op jit(solution)/shard_map/dot_general | solution.py:118
  137.2 2.7 %fusion.23 = bf16[128]{0:T(256)(128)(2,1)S(1)} fusion(bf16[128,768]{1,0:T(8,128)(2,1)} %get-tuple-element.9, bf16[1,768,2048]{2,1,0:T(8,128)(2,1)} %param.13, bf16[128,2048]{1,0:T(8,128)(2,1)} %bitcast.78), kind=kOutput, calls=%fused_computation.21 | convolution fusion | flops 403439488 | bytes 3866880 | tf_op jit(solution)/shard_map/dot_general | solution.py:58
  140.7 3.3 %all-to-all-start.8 = ((bf16[8,1,16]{2,1,0:T(2,128)(2,1)}), bf16[8,1,16]{2,1,0:T(2,128)(2,1)S(1)}, u32[]{:S(2)}, u32[]{:S(2)}) async-start(bf16[8,1,16]{2,1,0:T(2,128)(2,1)} %convert_element_type.154), calls=%async_computation.8 | async-start | bytes 8192 | tf_op jit(solution)/shard_map/all_to_all | solution.py:90
  144.0 1.3 multiply_convert_fusion
  145.3 3.1 %fusion.10 = f32[128,768]{1,0:T(8,128)S(1)} fusion(bf16[128,2048]{1,0:T(8,128)(2,1)S(1)} %bitcast.91, bf16[1,768,2048]{2,1,0:T(8,128)(2,1)} %param.13), kind=kOutput, calls=%fused_computation.11 | convolution fusion | flops 402653184 | bytes 4063232 | tf_op jit(solution)/shard_map/dot_general | solution.py:68
  149.6 2.0 fusion.19
  151.6 6.7 %all-to-all-start.6 = ((bf16[8,16,2048]{2,1,0:T(8,128)(2,1)}), bf16[8,16,2048]{2,1,0:T(8,128)(2,1)}, u32[]{:S(2)}, u32[]{:S(2)}) async-start(bf16[8,16,2048]{2,1,0:T(8,128)(2,1)} %bitcast.90), calls=%async_computation.6 | async-start | bytes 1048576 | tf_op jit(solution)/shard_map/all_to_all | solution.py:83
  159.1 17.2 %all-to-all-done.6 = bf16[8,16,2048]{2,1,0:T(8,128)(2,1)} async-done(((bf16[8,16,2048]{2,1,0:T(8,128)(2,1)}), bf16[8,16,2048]{2,1,0:T(8,128)(2,1)}, u32[]{:S(2)}, u32[]{:S(2)}) %all-to-all-start.6) | async-done | bytes 524320 | tf_op jit(solution)/shard_map/all_to_all | solution.py:83
  176.3 3.8 %all-to-all-start.9 = ((bf16[16,8,8]{1,2,0:T(8,128)(2,1)}), bf16[16,8,8]{1,2,0:T(8,128)(2,1)S(1)}, u32[]{:S(2)}, u32[]{:S(2)}) async-start(bf16[16,8,8]{1,2,0:T(8,128)(2,1)} %copy.47), calls=%async_computation.9 | async-start | bytes 65536 | tf_op jit(solution)/shard_map/all_to_all | solution.py:108
  180.1 2.2 fusion.22
  182.3 5.3 %all-to-all-done.9 = bf16[16,8,8]{1,2,0:T(8,128)(2,1)S(1)} async-done(((bf16[16,8,8]{1,2,0:T(8,128)(2,1)}), bf16[16,8,8]{1,2,0:T(8,128)(2,1)S(1)}, u32[]{:S(2)}, u32[]{:S(2)}) %all-to-all-start.9) | async-done | bytes 2080 | tf_op jit(solution)/shard_map/all_to_all | solution.py:108
  187.6 4.4 %all-to-all-start.7 = ((bf16[16,8,2048]{2,1,0:T(8,128)(2,1)}), bf16[16,8,2048]{2,1,0:T(8,128)(2,1)}, u32[]{:S(2)}, u32[]{:S(2)}) async-start(bf16[16,8,2048]{2,1,0:T(8,128)(2,1)} %fusion.22), calls=%async_computation.7 | async-start | bytes 1048576 | tf_op jit(solution)/shard_map/all_to_all | solution.py:107
  192.8 16.6 %all-to-all-done.7 = bf16[16,8,2048]{2,1,0:T(8,128)(2,1)} async-done(((bf16[16,8,2048]{2,1,0:T(8,128)(2,1)}), bf16[16,8,2048]{2,1,0:T(8,128)(2,1)}, u32[]{:S(2)}, u32[]{:S(2)}) %all-to-all-start.7) | async-done | bytes 524320 | tf_op jit(solution)/shard_map/all_to_all | solution.py:107
  209.4 1.7 reduce_sum.40
  211.1 1.9 bitcast_convert_fusion
  (41 shorter events, 7.7 us)
Async XLA Ops:
  7.2 110.1 %copy-start = (bf16[1,2048,768]{2,1,0:T(8,128)(2,1)S(1)}, bf16[1,2048,768]{2,1,0:T(8,128)(2,1)}, u32[]{:S(2)}) copy-start(bf16[1,2048,768]{2,1,0:T(8,128)(2,1)} %param.12) | copy-start | bytes 9437188
  9.6 24.9 %all-to-all-start = ((bf16[16,8,8]{2,1,0:T(8,128)(2,1)}), bf16[16,8,8]{2,1,0:T(8,128)(2,1)S(1)}, u32[]{:S(2)}, u32[]{:S(2)}) async-start(bf16[16,8,8]{2,1,0:T(8,128)(2,1)} %copy.39), calls=%async_computation | async-start | bytes 65536 | tf_op jit(solution)/shard_map/all_to_all | solution.py:26
  35.8 9.7 %all-to-all-start.1 = ((bf16[8,1,16]{2,1,0:T(2,128)(2,1)}), bf16[8,1,16]{2,1,0:T(2,128)(2,1)S(1)}, u32[]{:S(2)}, u32[]{:S(2)}) async-start(bf16[8,1,16]{2,1,0:T(2,128)(2,1)} %copy.43), calls=%async_computation.1 | async-start | bytes 8192 | tf_op jit(solution)/shard_map/all_to_all | solution.py:47
  68.4 20.3 %all-to-all-start.2 = ((bf16[16,8,2048]{2,1,0:T(8,128)(2,1)}), bf16[16,8,2048]{2,1,0:T(8,128)(2,1)}, u32[]{:S(2)}, u32[]{:S(2)}) async-start(bf16[16,8,2048]{2,1,0:T(8,128)(2,1)} %get-tuple-element.5), calls=%async_computation.2 | async-start | bytes 1048576 | tf_op jit(solution)/shard_map/all_to_all | solution.py:60
  88.7 21.5 %all-to-all-start.5 = ((bf16[8,16,2048]{2,1,0:T(8,128)(2,1)}), bf16[8,16,2048]{2,1,0:T(8,128)(2,1)}, u32[]{:S(2)}, u32[]{:S(2)}) async-start(bf16[8,16,2048]{2,1,0:T(8,128)(2,1)} %convolution_convert_fusion.1), calls=%async_computation.5 | async-start | bytes 1048576 | tf_op jit(solution)/shard_map/all_to_all | solution.py:46
  110.3 22.2 %all-to-all-start.3 = ((bf16[8,16,2048]{2,1,0:T(8,128)(2,1)}), bf16[8,16,2048]{2,1,0:T(8,128)(2,1)}, u32[]{:S(2)}, u32[]{:S(2)}) async-start(bf16[8,16,2048]{2,1,0:T(8,128)(2,1)} %convolution_convert_fusion.2), calls=%async_computation.3 | async-start | bytes 1048576 | tf_op jit(solution)/shard_map/all_to_all | solution.py:61
  114.4 96.7 %reduce-scatter.2.cloned.1.call-start = ((), (), s32[]{:S(2)}) async-start(), calls=%async_computation.11 | async-start | bytes 3538944 | tf_op jit(solution)/shard_map/reduce_scatter | solution.py:117
  140.7 10.9 %all-to-all-start.8 = ((bf16[8,1,16]{2,1,0:T(2,128)(2,1)}), bf16[8,1,16]{2,1,0:T(2,128)(2,1)S(1)}, u32[]{:S(2)}, u32[]{:S(2)}) async-start(bf16[8,1,16]{2,1,0:T(2,128)(2,1)} %convert_element_type.154), calls=%async_computation.8 | async-start | bytes 8192 | tf_op jit(solution)/shard_map/all_to_all | solution.py:90
  144.0 4.4 %copy-start.1 = (bf16[1,2048,768]{2,1,0:T(8,128)(2,1)S(1)}, bf16[1,2048,768]{2,1,0:T(8,128)(2,1)}, u32[]{:S(2)}) copy-start(bf16[1,2048,768]{2,1,0:T(8,128)(2,1)} %param.11) | copy-start | bytes 9437188
  144.0 4.4 %copy-start.2 = (f32[128,768]{1,0:T(8,128)S(1)}, f32[128,768]{1,0:T(8,128)}, u32[]{:S(2)}) copy-start(f32[128,768]{1,0:T(8,128)} %get-tuple-element.10) | copy-start | bytes 1179652
  151.6 40.4 %copy-start.3 = (s32[8,8]{1,0:T(8,128)S(1)}, s32[8,8]{1,0:T(8,128)}, u32[]{:S(2)}) copy-start(s32[8,8]{1,0:T(8,128)} %param.9) | copy-start | bytes 772
  151.6 24.7 %all-to-all-start.6 = ((bf16[8,16,2048]{2,1,0:T(8,128)(2,1)}), bf16[8,16,2048]{2,1,0:T(8,128)(2,1)}, u32[]{:S(2)}, u32[]{:S(2)}) async-start(bf16[8,16,2048]{2,1,0:T(8,128)(2,1)} %bitcast.90), calls=%async_computation.6 | async-start | bytes 1048576 | tf_op jit(solution)/shard_map/all_to_all | solution.py:83
  176.3 11.3 %all-to-all-start.9 = ((bf16[16,8,8]{1,2,0:T(8,128)(2,1)}), bf16[16,8,8]{1,2,0:T(8,128)(2,1)S(1)}, u32[]{:S(2)}, u32[]{:S(2)}) async-start(bf16[16,8,8]{1,2,0:T(8,128)(2,1)} %copy.47), calls=%async_computation.9 | async-start | bytes 65536 | tf_op jit(solution)/shard_map/all_to_all | solution.py:108
  187.6 21.8 %all-to-all-start.7 = ((bf16[16,8,2048]{2,1,0:T(8,128)(2,1)}), bf16[16,8,2048]{2,1,0:T(8,128)(2,1)}, u32[]{:S(2)}, u32[]{:S(2)}) async-start(bf16[16,8,2048]{2,1,0:T(8,128)(2,1)} %fusion.22), calls=%async_computation.7 | async-start | bytes 1048576 | tf_op jit(solution)/shard_map/all_to_all | solution.py:107
Sparse Core Ops, SparseCore 0:
  137.4 47.9 reduce-scatter.1
where the time goes:
time: 221 us; the launch traced here: 220 us
  waiting for transfers between devices  92.7 us (42%)
  starting transfers between devices  51.4 us (23%)
  matrix products  24.3 us (11%)
  blocking collectives  22.9 us (10%)
  between operations  14.2 us (6%)
  other arithmetic  11 us (5%)
  local copies, waits for them, and re-layouts  3.29 us (1%)
    all_to_all x1, blocking collectives, body(): lax.all_to_all(node_tokens, 'node', split_axis=0, concat_axis=0, tiled=True)  22.9 us
    all_to_all x1, starting transfers between devices, body(): lax.all_to_all(node_weights, 'node', split_axis=0, concat_axis=0, tiled=T...  17.4 us
    all_to_all x1, waiting for transfers between devices, body(): lax.all_to_all(row_grads.reshape(local_count, slot_count, model_width), '...  17.2 us
    all_to_all x1, waiting for transfers between devices, body(): lax.all_to_all(group_rows, 'node', split_axis=0, concat_axis=0, tiled=True)  16.6 us
    all_to_all x1, waiting for transfers between devices, body(): lax.all_to_all(pick_slots(got_tokens), 'local', split_axis=0, concat_axis...  15.3 us
    all_to_all x1, waiting for transfers between devices, body(): lax.all_to_all(node_grads, 'node', split_axis=0, concat_axis=0, tiled=True)  14 us
    all_to_all x1, waiting for transfers between devices, body(): lax.all_to_all(pick_slots(got_grads), 'local', split_axis=0, concat_axis=...  12.7 us
    all_to_all x1, waiting for transfers between devices, body(): lax.all_to_all(node_weights, 'node', split_axis=0, concat_axis=0, tiled=T...  7.07 us
  transfers between devices with their start and end apart: 10, of which 8 were waited for; matrix products, arithmetic and copies ran while one was open for 13% of the time, Pallas kernels for 0%

commit v1 on v0

v1 whole, which is shorter than its diff:
```python
import functools

import jax
import jax.numpy as jnp
from jax import lax
from jax.experimental import pallas as pl
from jax.experimental.pallas import tpu as pltpu
from jax.sharding import PartitionSpec as P

BF = jnp.bfloat16
F32 = jnp.float32
MESH = pl.DeviceIdType.MESH
LANES = 128
SLOT = 16
NT = (((1,), (1,)), ((), ()))


def near_first(count):
    return sorted(range(1, count), key=lambda j: (min(j, count - j), j))


def dot(a, b):
    return jnp.dot(a, b, preferred_element_type=F32)


def dot_nt(a, b):
    return lax.dot_general(a, b, NT, preferred_element_type=F32)


def kernel(
    sizes,
    tok_ref, cot_ref, ids_ref, rw_ref, wg_hbm, wu_hbm, wd_hbm,
    tg_ref, wgrad_ref, dg_ref,
    wg, wu, wd,
    col_t, col_c, sel_ref, selt_ref,
    send_t, recv_t, send_c, recv_c,
    fac_a, fac_b, hid, hid_t, out_g, gate_g, up_g, eo,
    send_b, recv_b, group, other, summed, home,
    rs_send, rs_recv,
    w_sem, xs_sem, xr_sem, fs_sem, ys_sem, yr_sem, zs_sem, zr_sem, cx_sem, hs_sem, hr_sem,
):
    nz, nn, nl = sizes
    nx = nn // 2
    toks, width = tok_ref.shape
    top = ids_ref.shape[1]
    half = width // 2
    quarter = width // 4
    hidden_units = wd.shape[0]
    chunk = hidden_units // nz
    slots = nl * SLOT
    rows = nn * SLOT
    tile = min(256, hidden_units)
    wide = min(256, half)

    z = lax.axis_index("edata")
    n = lax.axis_index("node")
    l = lax.axis_index("local")
    core = lax.rem(n, 2)
    x = lax.div(n, 2)
    mate = n + 1 - 2 * core
    expert = n * nl + l

    def node_at(j):
        return lax.rem(n + 2 * j, nn)

    def local_at(j):
        return lax.rem(l + j, nl)

    weights = [
        pltpu.make_async_copy(hbm.at[0], vmem, w_sem.at[i])
        for i, (hbm, vmem) in enumerate(((wg_hbm, wg), (wu_hbm, wu), (wd_hbm, wd)))
    ]
    for copy in weights:
        copy.start()

    barrier = pltpu.get_barrier_semaphore()
    for j in range(1, nx):
        pl.semaphore_signal(barrier, inc=1, device_id={"node": node_at(j)}, device_id_type=MESH)
    pl.semaphore_signal(barrier, inc=1, device_id={"node": mate}, device_id_type=MESH)
    for j in range(1, nl):
        pl.semaphore_signal(barrier, inc=1, device_id={"local": local_at(j)}, device_id_type=MESH)
    z_next = lax.rem(z + 1, nz)
    z_prev = lax.rem(z + nz - 1, nz)
    for peer in (z_next, z_prev):
        pl.semaphore_signal(barrier, inc=1, device_id={"edata": peer}, device_id_type=MESH)

    ids = ids_ref[...]
    lane = lax.broadcasted_iota(jnp.int32, (toks, LANES), 1)
    dense = jnp.zeros((toks, LANES), F32)
    for k in range(top):
        dense = dense + jnp.where(
            ids[:, k : k + 1] == lane, rw_ref[:, k : k + 1].astype(F32), 0.0
        )
    tok = tok_ref[...].astype(F32)
    cot = cot_ref[...].astype(F32)
    col_t[n, :, :half] = jnp.concatenate([tok[:, :half], tok[:, half:]], axis=0).astype(BF)
    col_t[n, :, half:] = jnp.concatenate([dense, jnp.zeros_like(dense)], axis=0).astype(BF)
    col_c[n, :, :] = jnp.concatenate([cot[:, :half], cot[:, half:]], axis=0).astype(BF)

    pl.semaphore_wait(barrier, nx - 1 + 1 + nl - 1 + 2)

    started = []

    def x_copy(which, src, target, send_sem):
        buf = (col_t, col_c)[which]
        return pltpu.make_async_remote_copy(
            src_ref=buf.at[src], dst_ref=buf.at[src],
            send_sem=send_sem, recv_sem=xr_sem.at[which, src],
            device_id={"node": target}, device_id_type=MESH,
        )

    order_x = near_first(nx)
    for which in range(2):
        for j in order_x:
            copy = x_copy(which, n, node_at(j), xs_sem.at[which, j])
            copy.start()
            started.append(copy)
        copy = x_copy(which, n, mate, xs_sem.at[which, 0])
        copy.start()
        started.append(copy)

    def spread(which):
        for j in order_x:
            src = node_at(nx - j)
            x_copy(which, src, mate, fs_sem.at[which, j]).wait_recv()
            copy = x_copy(which, src, mate, fs_sem.at[which, j])
            copy.start()
            started.append(copy)
        for j in [0] + order_x:
            src = lax.rem(mate + 2 * (nx - j), nn)
            x_copy(which, src, mate, fs_sem.at[which, j]).wait_recv()

    def y_copy(kind, src_buf, dst_buf, row, j, cols):
        return pltpu.make_async_remote_copy(
            src_ref=src_buf.at[pl.ds(pl.multiple_of(row * SLOT, SLOT), SLOT), cols],
            dst_ref=dst_buf.at[pl.ds(pl.multiple_of(l * SLOT, SLOT), SLOT), cols],
            send_sem=ys_sem.at[kind, j], recv_sem=yr_sem.at[kind, l],
            device_id={"local": row}, device_id_type=MESH,
        )

    order_y = near_first(nl)

    def y_send(kind, src_buf, dst_buf, cols):
        for j in order_y:
            copy = y_copy(kind, src_buf, dst_buf, local_at(j), j, cols)
            copy.start()
            started.append(copy)
        mine = pl.ds(pl.multiple_of(l * SLOT, SLOT), SLOT)
        dst_buf[mine, cols] = src_buf[mine, cols]

    def y_wait(kind, dst_buf, cols):
        for j in order_y:
            src = local_at(nl - j)
            part = dst_buf.at[pl.ds(pl.multiple_of(src * SLOT, SLOT), SLOT), cols]
            pltpu.make_async_remote_copy(
                src_ref=part, dst_ref=part, send_sem=ys_sem.at[kind, j],
                recv_sem=yr_sem.at[kind, src], device_id={"local": src}, device_id_type=MESH,
            ).wait_recv()

    left, right = slice(0, half), slice(half, width)
    right_ext = slice(half, width + LANES)
    all_ext = slice(0, width + LANES)

    spread(0)
    col_w = col_t[:, :, half:].reshape(rows, LANES)
    slot_id = lax.broadcasted_iota(jnp.int32, (slots, LANES), 0)
    lane_id = lax.broadcasted_iota(jnp.int32, (slots, LANES), 1)
    names = (lane_id == n * nl + lax.div(slot_id, SLOT)).astype(F32).astype(BF)
    named = dot_nt(names, col_w) != 0.0
    below = (
        lax.broadcasted_iota(jnp.int32, (rows, rows), 1)
        <= lax.broadcasted_iota(jnp.int32, (rows, rows), 0)
    ).astype(F32).astype(BF)
    count = dot_nt(named.astype(F32).astype(BF), below)
    place = lax.rem(lax.broadcasted_iota(jnp.int32, (slots, rows), 0), SLOT).astype(F32)
    sel0 = jnp.where(named & (count == place + 1.0), 1.0, 0.0)
    sel = jnp.concatenate([sel0, pltpu.roll(sel0, toks, 1)], axis=0)
    sel_ref[...] = sel.astype(BF)

    def pick(src_col, dst):
        for at in range(0, half, wide):
            got = dot(sel_ref[...], src_col[:, :, at : at + wide].reshape(rows, wide)).astype(BF)
            dst[:, at : at + wide] = got[:slots]
            dst[:, half + at : half + at + wide] = got[slots:]

    pick(col_t, send_t)
    send_t[:, width:] = dot(sel_ref[:slots, :], col_w).astype(BF)
    y_send(0, send_t, recv_t, all_ext)
    selt_ref[...] = sel.T.astype(BF)

    spread(1)
    pick(col_c, send_c)
    y_send(1, send_c, recv_c, left)
    y_send(2, send_c, recv_c, right)

    weights[0].wait()
    weights[1].wait()
    y_wait(0, recv_t, all_ext)
    for at in range(0, hidden_units, tile):
        cols = slice(at, at + tile)
        gate = dot(recv_t[:, :width], wg[:, cols])
        up = dot(recv_t[:, :width], wu[:, cols])
        sig = jax.nn.sigmoid(gate)
        silu = gate * sig
        fac_a[:, cols] = up * sig * (1.0 + gate * (1.0 - sig))
        fac_b[:, cols] = silu
        hidden = silu * up
        hid[:, cols] = hidden.astype(BF)
        hid_t[cols, :] = hidden.T.astype(BF)
    row_lane = lax.broadcasted_iota(jnp.int32, (slots, LANES), 1)
    scale = jnp.sum(
        jnp.where(row_lane == expert, recv_t[:, width:].astype(F32), 0.0), axis=1, keepdims=True
    )

    def scale_grads(cols):
        out_g[:, cols] = (scale * recv_c[:, cols].astype(F32)).astype(BF)

    def z_step(stream, step):
        ahead = stream % 2 == 0
        cols = slice(stream * quarter, (stream + 1) * quarter)
        part = lax.rem(z + 2 * nz - 1 - step, nz) if ahead else lax.rem(z + 1 + step, nz)

        def z_copy(at):
            return pltpu.make_async_remote_copy(
                src_ref=rs_send.at[stream, at], dst_ref=rs_recv.at[stream, at],
                send_sem=zs_sem.at[stream, at], recv_sem=zr_sem.at[stream, at],
                device_id={"edata": z_next if ahead else z_prev}, device_id_type=MESH,
            )

        own = dot(hid_t[pl.ds(pl.multiple_of(part * chunk, SLOT), chunk), :], out_g[:, cols])
        if step > 0:
            z_copy(step - 1).wait_recv()
            own = own + rs_recv[stream, step - 1].astype(F32)
        if step < nz - 1:
            rs_send[stream, step] = own.astype(BF)
            copy = z_copy(step)
            copy.start()
            started.append(copy)
        else:
            dg_ref[0, :, cols] = own

    y_wait(1, recv_c, left)
    scale_grads(left)
    z_step(0, 0)
    z_step(1, 0)
    y_wait(2, recv_c, right)
    scale_grads(right)
    z_step(2, 0)
    z_step(3, 0)

    weights[2].wait()
    for at in range(0, hidden_units, tile):
        cols = slice(at, at + tile)
        grad = dot_nt(out_g[...], wd[cols, :])
        gate_g[:, cols] = (grad * fac_a[:, cols]).astype(BF)
        up_g[:, cols] = (grad * fac_b[:, cols]).astype(BF)

    def row_grads(cols):
        for at in range(cols.start, cols.stop, wide):
            feats = slice(at, at + wide)
            send_b[:, feats] = (
                dot_nt(gate_g[...], wg[feats, :]) + dot_nt(up_g[...], wu[feats, :])
            ).astype(BF)

    pending = [(step, stream) for step in range(1, nz + 0) for stream in range(4)]

    def z_advance(count):
        for _ in range(count):
            if pending:
                step, stream = pending.pop(0)
                z_step(stream, step)

    row_grads(left)
    y_send(3, send_b, recv_b, left)
    z_advance(2)
    row_grads(right)
    weight_sum = jnp.zeros((slots, 1), F32)
    for at in range(0, width, wide):
        feats = slice(at, at + wide)
        out = dot(hid[...], wd[:, feats])
        weight_sum = weight_sum + jnp.sum(
            recv_c[:, feats].astype(F32) * out, axis=1, keepdims=True
        )
    send_b[:, width:] = jnp.where(row_lane == expert, weight_sum, 0.0).astype(BF)
    y_send(4, send_b, recv_b, right_ext)
    z_advance(10)

    y_wait(3, recv_b, left)
    y_wait(4, recv_b, right_ext)
    for at in range(0, half, wide):
        got = dot(selt_ref[:, :slots], recv_b[:, at : at + wide]) + dot(
            selt_ref[:, slots:], recv_b[:, half + at : half + at + wide]
        )
        group[:, :, :, at : at + wide] = got.astype(BF).reshape(nx, 2, SLOT, wide)
    group[:, :, :, half:] = (
        dot(selt_ref[:, :slots], recv_b[:, width:]).astype(BF).reshape(nx, 2, SLOT, LANES)
    )
    swap = pltpu.make_async_remote_copy(
        src_ref=group.at[:, 1 - core], dst_ref=other, send_sem=cx_sem.at[0], recv_sem=cx_sem.at[1],
        device_id={"node": mate}, device_id_type=MESH,
    )
    swap.start()
    z_advance(4)
    swap.wait()
    summed[...] = (group[:, core].astype(F32) + other[...].astype(F32)).astype(BF)

    def h_copy(target, j):
        return pltpu.make_async_remote_copy(
            src_ref=summed.at[target], dst_ref=home.at[x], send_sem=hs_sem.at[j],
            recv_sem=hr_sem.at[x], device_id={"node": 2 * target + core}, device_id_type=MESH,
        )

    for j in order_x:
        copy = h_copy(lax.rem(x + j, nx), j)
        copy.start()
        started.append(copy)
    home[x] = summed[x]
    z_advance(4)
    for j in order_x:
        src = lax.rem(x + nx - j, nx)
        pltpu.make_async_remote_copy(
            src_ref=home.at[src], dst_ref=home.at[src], send_sem=hs_sem.at[j],
            recv_sem=hr_sem.at[src], device_id={"node": 2 * src + core}, device_id_type=MESH,
        ).wait_recv()
    total = jnp.sum(home[...].astype(F32), axis=0)
    tg_ref[:, :half] = total[:toks, :half].astype(BF)
    tg_ref[:, half:] = total[toks:, :half].astype(BF)
    weight_dense = total[:toks, half:]
    slot_lane = lax.broadcasted_iota(jnp.int32, (toks, top), 1)
    weight_out = jnp.zeros((toks, top), F32)
    for k in range(top):
        value = jnp.sum(
            jnp.where(ids[:, k : k + 1] == lane, weight_dense, 0.0), axis=1, keepdims=True
        )
        weight_out = jnp.where(slot_lane == k, value, weight_out)
    wgrad_ref[...] = weight_out.astype(BF)
    z_advance(len(pending))
    for copy in started:
        copy.wait_send()


def body(tokens, cotangent, expert_ids, route_weights, w_gate, w_up, w_down):
    nz, nn, nl = (lax.axis_size(name) for name in ("edata", "node", "local"))
    nx = nn // 2
    toks, width = tokens.shape
    top = expert_ids.shape[1]
    hidden_units = w_gate.shape[2]
    half, quarter, chunk = width // 2, width // 4, hidden_units // nz
    slots, rows = nl * SLOT, nn * SLOT
    vmem = pl.BlockSpec(memory_space=pltpu.VMEM)
    hbm = pl.BlockSpec(memory_space=pl.ANY)
    dma = pltpu.SemaphoreType.DMA
    return pl.pallas_call(
        functools.partial(kernel, (nz, nn, nl)),
        out_shape=(
            jax.ShapeDtypeStruct((toks, width), BF),
            jax.ShapeDtypeStruct((toks, top), BF),
            jax.ShapeDtypeStruct((1, chunk, width), F32),
        ),
        in_specs=[vmem, vmem, vmem, vmem, hbm, hbm, hbm],
        out_specs=(vmem, vmem, vmem),
        scratch_shapes=[
            pltpu.VMEM((width, hidden_units), BF),
            pltpu.VMEM((width, hidden_units), BF),
            pltpu.VMEM((hidden_units, width), BF),
            pltpu.VMEM((nn, SLOT, half + LANES), BF),
            pltpu.VMEM((nn, SLOT, half), BF),
            pltpu.VMEM((2 * slots, rows), BF),
            pltpu.VMEM((rows, 2 * slots), BF),
            pltpu.VMEM((slots, width + LANES), BF),
            pltpu.VMEM((slots, width + LANES), BF),
            pltpu.VMEM((slots, width), BF),
            pltpu.VMEM((slots, width), BF),
            pltpu.VMEM((slots, hidden_units), F32),
            pltpu.VMEM((slots, hidden_units), F32),
            pltpu.VMEM((slots, hidden_units), BF),
            pltpu.VMEM((hidden_units, slots), BF),
            pltpu.VMEM((slots, width), BF),
            pltpu.VMEM((slots, hidden_units), BF),
            pltpu.VMEM((slots, hidden_units), BF),
            pltpu.VMEM((8, LANES), F32),
            pltpu.VMEM((slots, width + LANES), BF),
            pltpu.VMEM((slots, width + LANES), BF),
            pltpu.VMEM((nx, 2, SLOT, half + LANES), BF),
            pltpu.VMEM((nx, SLOT, half + LANES), BF),
            pltpu.VMEM((nx, SLOT, half + LANES), BF),
            pltpu.VMEM((nx, SLOT, half + LANES), BF),
            pltpu.VMEM((4, nz - 1, chunk, quarter), BF),
            pltpu.VMEM((4, nz - 1, chunk, quarter), BF),
            dma((3,)),
            dma((2, nx)),
            dma((2, nn)),
            dma((2, nx)),
            dma((5, nl)),
            dma((5, nl)),
            dma((4, nz - 1)),
            dma((4, nz - 1)),
            dma((2,)),
            dma((nx,)),
            dma((nx,)),
        ],
        compiler_params=pltpu.CompilerParams(
            collective_id=0, has_side_effects=True, vmem_limit_bytes=48 * 1024 * 1024
        ),
        name="expert_layer",
    )(tokens, cotangent, expert_ids, route_weights, w_gate, w_up, w_down)


def solution(mesh):
    in_specs = (
        P(("edata", "node", "local"), None),
        P(("edata", "node", "local"), None),
        P(("edata", "node", "local"), None),
        P(("edata", "node", "local"), None),
        P(("node", "local"), None, None),
        P(("node", "local"), None, None),
        P(("node", "local"), None, None),
    )
    out_specs = (
        P(("edata", "node", "local"), None),
        P(("edata", "node", "local"), None),
        P(("node", "local"), "edata", None),
    )
    return jax.shard_map(body, mesh=mesh, in_specs=in_specs, out_specs=out_specs, check_vma=False)
```

time: 221 us -> 108 us (0.49)
  the two profiles are of different devices: /device:TPU:1 before, /device:TPU:12 now
where the time goes in v1:
time: 108 us
  Pallas kernels  100 us (93%)
  local copies, waits for them, and re-layouts  6.84 us (6%)
    pallas_call x1, Pallas kernels, body(): pl.pallas_call(functools.partial(kernel, (nz, nn, nl)), out_shape=(jax.Sh...  100 us
    unnamed x13, local copies, waits for them, and re-layouts  6.84 us

profile of v1, /device:TPU:12, one launch (start us, length us, event | category | flops | bytes accessed | tf_op | source)
XLA Modules:
  0.0 107.8 jit_solution(14204811927092739370)
XLA Ops:
  0.6 0.0 copy-start
  0.6 1.9 %copy-done = bf16[1,2048,768]{2,1,0:T(8,128)(2,1)S(1)} copy-done((bf16[1,2048,768]{2,1,0:T(8,128)(2,1)S(1)}, bf16[1,2048,768]{2,1,0:T(8,128)(2,1)}, u32[]{:S(2)}) %copy-start) | copy-done | bytes 3145752
  2.5 0.0 copy-start.1
  2.5 0.8 copy-done.1
  3.3 0.0 copy-start.2
  3.3 0.8 copy-done.2
  4.0 0.0 copy-start.3
  4.0 0.7 copy-done.3
  4.7 0.0 copy-start.4
  4.7 0.7 copy-done.4
  5.4 100.3 %expert_layer.1 = (bf16[8,2048]{1,0:T(8,128)(2,1)S(1)}, bf16[8,8]{1,0:T(8,128)(2,1)S(1)}, f32[1,96,2048]{2,1,0:T(8,128)S(1)}) custom-call(bf16[8,2048]{1,0:T(8,128)(2,1)S(1)} %copy-done.1, bf16[8,2048]{1,0:T(8,128)(2,1)S(1)} %copy-done.2, s32[8,8]{1,0:T(8,128)S(1)} %copy-done.3, bf16[8,8]{1,0:T(8,128)(2,1)S(1)} %copy-done.4, ...), custom_call_target="tpu_custom_call" | custom-call | tf_op jit(solution)/shard_map/expert_layer/pallas_call | solution.py:353
  105.7 0.6 copy.13
  106.3 0.6 copy.14
  106.9 0.9 copy.15
Async XLA Ops:
  0.6 1.9 %copy-start = (bf16[1,2048,768]{2,1,0:T(8,128)(2,1)S(1)}, bf16[1,2048,768]{2,1,0:T(8,128)(2,1)}, u32[]{:S(2)}) copy-start(bf16[1,2048,768]{2,1,0:T(8,128)(2,1)} %wg_hbm.1) | copy-start | bytes 9437188
  2.5 0.8 copy-start.1
  3.3 0.8 copy-start.2
  4.0 0.7 copy-start.3
  4.7 0.7 copy-start.4

commit v2 on v1

v2 whole, which is shorter than its diff:
```python
import functools

import jax
import jax.numpy as jnp
from jax import lax
from jax.experimental import pallas as pl
from jax.experimental.pallas import tpu as pltpu
from jax.sharding import PartitionSpec as P

BF = jnp.bfloat16
F32 = jnp.float32
MESH = pl.DeviceIdType.MESH
LANES = 128
SLOT = 16
NT = (((1,), (1,)), ((), ()))


def near_first(count):
    return sorted(range(1, count), key=lambda j: (min(j, count - j), j))


def dot(a, b):
    return jnp.dot(a, b, preferred_element_type=F32)


def dot_nt(a, b):
    return lax.dot_general(a, b, NT, preferred_element_type=F32)


def kernel(
    sizes,
    tok_hbm, cot_hbm, ids_hbm, rw_hbm, wg_hbm, wu_hbm, wd_hbm,
    tg_ref, wgrad_ref, dg_ref,
    tok_ref, cot_ref, ids_ref, rw_ref, wg, wu, wd,
    col_t, col_c, sel_ref, selt_ref,
    send_t, recv_t, send_c, recv_c,
    fac_a, fac_b, hid, hid_t, out_g, gate_g, up_g, hid_g,
    send_b, recv_b, group, other, summed, home,
    partial, rs_send, rs_recv,
    w_sem, xs_sem, xr_sem, fs_sem, ys_sem, yr_sem, zs_sem, zr_sem, cx_sem, hs_sem, hr_sem,
):
    nz, nn, nl = sizes
    nx = nn // 2
    toks, width = tok_ref.shape
    top = ids_ref.shape[1]
    half = width // 2
    quarter = width // 4
    lead = half // 4
    hidden_units = wd.shape[0]
    chunk = hidden_units // nz
    slots = nl * SLOT
    rows = nn * SLOT
    tile = min(256, hidden_units)
    wide = min(256, half)

    z = lax.axis_index("edata")
    n = lax.axis_index("node")
    l = lax.axis_index("local")
    core = lax.rem(n, 2)
    x = lax.div(n, 2)
    mate = n + 1 - 2 * core
    expert = n * nl + l

    def node_at(j):
        return lax.rem(n + 2 * j, nn)

    def local_at(j):
        return lax.rem(l + j, nl)

    inputs = [
        pltpu.make_async_copy(hbm, vmem, w_sem.at[i])
        for i, (hbm, vmem) in enumerate((
            (ids_hbm, ids_ref), (rw_hbm, rw_ref), (tok_hbm, tok_ref), (cot_hbm, cot_ref),
            (wg_hbm.at[0], wg), (wu_hbm.at[0], wu), (wd_hbm.at[0], wd),
        ))
    ]
    for copy in inputs:
        copy.start()
    weights = inputs[4:]

    barrier = pltpu.get_barrier_semaphore()
    for j in range(1, nx):
        pl.semaphore_signal(barrier, inc=1, device_id={"node": node_at(j)}, device_id_type=MESH)
    pl.semaphore_signal(barrier, inc=1, device_id={"node": mate}, device_id_type=MESH)
    for j in range(1, nl):
        pl.semaphore_signal(barrier, inc=1, device_id={"local": local_at(j)}, device_id_type=MESH)
    z_next = lax.rem(z + 1, nz)
    z_prev = lax.rem(z + nz - 1, nz)
    for peer in (z_next, z_prev):
        pl.semaphore_signal(barrier, inc=1, device_id={"edata": peer}, device_id_type=MESH)

    for copy in inputs[:4]:
        copy.wait()
    ids = ids_ref[...]
    lane = lax.broadcasted_iota(jnp.int32, (toks, LANES), 1)
    dense = jnp.zeros((toks, LANES), F32)
    for k in range(top):
        dense = dense + jnp.where(
            ids[:, k : k + 1] == lane, rw_ref[:, k : k + 1].astype(F32), 0.0
        )
    tok = tok_ref[...].astype(F32)
    cot = cot_ref[...].astype(F32)
    col_t[n, :, LANES:] = jnp.concatenate([tok[:, :half], tok[:, half:]], axis=0).astype(BF)
    col_t[n, :, :LANES] = jnp.concatenate([dense, jnp.zeros_like(dense)], axis=0).astype(BF)
    col_c[n, :, :] = jnp.concatenate([cot[:, :half], cot[:, half:]], axis=0).astype(BF)

    pl.semaphore_wait(barrier, nx - 1 + 1 + nl - 1 + 2)

    started = []

    x_parts = [
        col_t.at[:, :, : LANES + lead],
        col_t.at[:, :, LANES + lead :],
        col_c,
    ]

    def x_copy(which, src, target, send_sem):
        block = x_parts[which].at[src]
        return pltpu.make_async_remote_copy(
            src_ref=block, dst_ref=block,
            send_sem=send_sem, recv_sem=xr_sem.at[which, src],
            device_id={"node": target}, device_id_type=MESH,
        )

    order_x = near_first(nx)

    def x_send(which):
        for j in order_x:
            copy = x_copy(which, n, node_at(j), xs_sem.at[which, j])
            copy.start()
            started.append(copy)
        copy = x_copy(which, n, mate, xs_sem.at[which, 0])
        copy.start()
        started.append(copy)

    def spread(which):
        for j in order_x:
            src = node_at(nx - j)
            x_copy(which, src, mate, fs_sem.at[which, j]).wait_recv()
            copy = x_copy(which, src, mate, fs_sem.at[which, j])
            copy.start()
            started.append(copy)
        for j in [0] + order_x:
            src = lax.rem(mate + 2 * (nx - j), nn)
            x_copy(which, src, mate, fs_sem.at[which, j]).wait_recv()

    x_send(0)
    x_send(1)

    def y_copy(kind, src_buf, dst_buf, row, j, cols):
        return pltpu.make_async_remote_copy(
            src_ref=src_buf.at[pl.ds(pl.multiple_of(row * SLOT, SLOT), SLOT), cols],
            dst_ref=dst_buf.at[pl.ds(pl.multiple_of(l * SLOT, SLOT), SLOT), cols],
            send_sem=ys_sem.at[kind, j], recv_sem=yr_sem.at[kind, l],
            device_id={"local": row}, device_id_type=MESH,
        )

    order_y = near_first(nl)

    def y_send(kind, src_buf, dst_buf, cols):
        for j in order_y:
            copy = y_copy(kind, src_buf, dst_buf, local_at(j), j, cols)
            copy.start()
            started.append(copy)
        mine = pl.ds(pl.multiple_of(l * SLOT, SLOT), SLOT)
        dst_buf[mine, cols] = src_buf[mine, cols]

    def y_wait(kind, dst_buf, cols):
        for j in order_y:
            src = local_at(nl - j)
            part = dst_buf.at[pl.ds(pl.multiple_of(src * SLOT, SLOT), SLOT), cols]
            pltpu.make_async_remote_copy(
                src_ref=part, dst_ref=part, send_sem=ys_sem.at[kind, j],
                recv_sem=yr_sem.at[kind, src], device_id={"local": src}, device_id_type=MESH,
            ).wait_recv()

    parts = [slice(i * quarter, (i + 1) * quarter) for i in (0, 2, 1, 3)]
    back_parts = parts[:3] + [slice(parts[3].start, width + LANES)]
    lead_cols, rest_cols = slice(0, LANES + 2 * lead), slice(LANES + 2 * lead, LANES + width)

    spread(0)
    col_w = col_t[:, :, :LANES].reshape(rows, LANES)
    slot_id = lax.broadcasted_iota(jnp.int32, (slots, LANES), 0)
    lane_id = lax.broadcasted_iota(jnp.int32, (slots, LANES), 1)
    names = (lane_id == n * nl + lax.div(slot_id, SLOT)).astype(F32).astype(BF)
    named = dot_nt(names, col_w) != 0.0
    below = (
        lax.broadcasted_iota(jnp.int32, (rows, rows), 1)
        <= lax.broadcasted_iota(jnp.int32, (rows, rows), 0)
    ).astype(F32).astype(BF)
    count = dot_nt(named.astype(F32).astype(BF), below)
    place = lax.rem(lax.broadcasted_iota(jnp.int32, (slots, rows), 0), SLOT).astype(F32)
    sel0 = jnp.where(named & (count == place + 1.0), 1.0, 0.0)
    sel = jnp.concatenate([sel0, pltpu.roll(sel0, toks, 1)], axis=0)
    sel_ref[...] = sel.astype(BF)

    def pick(src_col, at, size, dst, first, second):
        for i in range(0, size, lead):
            got = src_col[:, :, at + i : at + i + lead].reshape(rows, lead)
            got = dot(sel_ref[...], got).astype(BF)
            dst[:, first + i : first + i + lead] = got[:slots]
            dst[:, second + i : second + i + lead] = got[slots:]

    send_t[:, :LANES] = dot(sel_ref[:slots, :], col_w).astype(BF)
    pick(col_t, LANES, lead, send_t, LANES, LANES + lead)
    y_send(0, send_t, recv_t, lead_cols)
    spread(1)
    x_send(2)
    rest = half - lead
    pick(col_t, LANES + lead, rest, send_t, LANES + 2 * lead, LANES + 2 * lead + rest)
    y_send(9, send_t, recv_t, rest_cols)
    selt_ref[...] = sel.T.astype(BF)

    spread(2)
    pick(col_c, 0, quarter, send_c, 0, half)
    y_send(1, send_c, recv_c, parts[0])
    y_send(2, send_c, recv_c, parts[1])
    pick(col_c, quarter, quarter, send_c, quarter, half + quarter)
    y_send(3, send_c, recv_c, parts[2])
    y_send(4, send_c, recv_c, parts[3])

    weights[0].wait()
    weights[1].wait()
    y_wait(0, recv_t, lead_cols)
    y_wait(9, recv_t, rest_cols)
    row_parts = [
        (LANES, 0, lead),
        (LANES + lead, half, lead),
        (LANES + 2 * lead, lead, rest),
        (LANES + 2 * lead + rest, half + lead, rest),
    ]
    for at in range(0, hidden_units, tile):
        cols = slice(at, at + tile)
        gate = jnp.zeros((slots, tile), F32)
        up = jnp.zeros((slots, tile), F32)
        for first, feat, size in row_parts:
            got = recv_t[:, first : first + size]
            gate = gate + dot(got, wg[feat : feat + size, cols])
            up = up + dot(got, wu[feat : feat + size, cols])
        sig = jax.nn.sigmoid(gate)
        silu = gate * sig
        fac_a[:, cols] = up * sig * (1.0 + gate * (1.0 - sig))
        fac_b[:, cols] = silu
        hidden = silu * up
        hid[:, cols] = hidden.astype(BF)
        hid_t[cols, :] = hidden.T.astype(BF)
    row_lane = lax.broadcasted_iota(jnp.int32, (slots, LANES), 1)
    scale = jnp.sum(
        jnp.where(row_lane == expert, recv_t[:, :LANES].astype(F32), 0.0), axis=1, keepdims=True
    )
    weights[2].wait()

    def z_step(stream, step):
        ahead = stream % 2 == 0
        cols = parts[stream]
        part = lax.rem(z + 2 * nz - 1 - step, nz) if ahead else lax.rem(z + 1 + step, nz)
        own = partial.at[pl.ds(pl.multiple_of(part * chunk, SLOT), chunk), cols]

        def z_copy(at):
            return pltpu.make_async_remote_copy(
                src_ref=own if at == 0 else rs_send.at[stream, at - 1], dst_ref=rs_recv.at[stream, at],
                send_sem=zs_sem.at[stream, at], recv_sem=zr_sem.at[stream, at],
                device_id={"edata": z_next if ahead else z_prev}, device_id_type=MESH,
            )

        if step > 0:
            z_copy(step - 1).wait_recv()
        if step == nz - 1:
            dg_ref[0, :, cols] = rs_recv[stream, step - 1].astype(F32) + own[...].astype(F32)
            return
        if step > 0:
            rs_send[stream, step - 1] = rs_recv[stream, step - 1] + own[...]
        copy = z_copy(step)
        copy.start()
        started.append(copy)

    done = [0] * 4

    def z_advance(upto, streams=(0, 1, 2, 3)):
        for step in range(min(upto, nz)):
            for stream in streams:
                if done[stream] == step:
                    z_step(stream, step)
                    done[stream] += 1

    weight_sum = jnp.zeros((slots, 1), F32)
    for i, cols in enumerate(parts):
        y_wait(1 + i, recv_c, cols)
        out_g[:, cols] = (scale * recv_c[:, cols].astype(F32)).astype(BF)
        for at in range(0, hidden_units, tile):
            units = slice(at, at + tile)
            partial[units, cols] = dot(hid_t[units, :], out_g[:, cols]).astype(BF)
        z_advance(1, (i,))
        if i == 2:
            z_advance(2, (0,))
        if i == 3:
            z_advance(2, (1,))
        for at in range(0, hidden_units, tile):
            units = slice(at, at + tile)
            grad = dot_nt(out_g[:, cols], wd[units, cols])
            if i > 0:
                grad = grad + hid_g[:, units]
            if i < 3:
                hid_g[:, units] = grad
            else:
                gate_g[:, units] = (grad * fac_a[:, units]).astype(BF)
                up_g[:, units] = (grad * fac_b[:, units]).astype(BF)
        out = dot(hid[...], wd[:, cols])
        weight_sum = weight_sum + jnp.sum(
            recv_c[:, cols].astype(F32) * out, axis=1, keepdims=True
        )

    for i, cols in enumerate(parts):
        for at in range(cols.start, cols.stop, min(wide, quarter)):
            feats = slice(at, at + min(wide, quarter))
            send_b[:, feats] = (
                dot_nt(gate_g[...], wg[feats, :]) + dot_nt(up_g[...], wu[feats, :])
            ).astype(BF)
        if i == 3:
            send_b[:, width:] = jnp.where(row_lane == expert, weight_sum, 0.0).astype(BF)
        y_send(5 + i, send_b, recv_b, back_parts[i])
        if i == 0:
            z_advance(2)
        if i == 2:
            z_advance(3)
    z_advance(4)

    home_cols = [slice(0, quarter), slice(quarter, half + LANES)]

    def gather_group(i):
        y_wait(5 + 2 * i, recv_b, back_parts[2 * i])
        y_wait(6 + 2 * i, recv_b, back_parts[2 * i + 1])
        at, end = i * quarter, (i + 1) * quarter
        got = dot(selt_ref[:, :slots], recv_b[:, at:end]) + dot(
            selt_ref[:, slots:], recv_b[:, half + at : half + end]
        )
        group[:, :, :, at:end] = got.astype(BF).reshape(nx, 2, SLOT, quarter)
        if i == 1:
            group[:, :, :, half:] = (
                dot(selt_ref[:, :slots], recv_b[:, width:]).astype(BF).reshape(nx, 2, SLOT, LANES)
            )
        cols = home_cols[i]
        swap = pltpu.make_async_remote_copy(
            src_ref=group.at[:, 1 - core, :, cols], dst_ref=other.at[:, :, cols],
            send_sem=cx_sem.at[i, 0], recv_sem=cx_sem.at[i, 1],
            device_id={"node": mate}, device_id_type=MESH,
        )
        swap.start()
        return swap

    def send_home(i, swap):
        cols = home_cols[i]
        swap.wait()
        summed[:, :, cols] = (
            group[:, core, :, cols].astype(F32) + other[:, :, cols].astype(F32)
        ).astype(BF)
        for j in order_x:
            target = lax.rem(x + j, nx)
            copy = pltpu.make_async_remote_copy(
                src_ref=summed.at[target, :, cols], dst_ref=home.at[x, :, cols],
                send_sem=hs_sem.at[i, j], recv_sem=hr_sem.at[i, x],
                device_id={"node": 2 * target + core}, device_id_type=MESH,
            )
            copy.start()
            started.append(copy)
        home[x, :, cols] = summed[x, :, cols]

    def home_sum(i):
        cols = home_cols[i]
        for j in order_x:
            src = lax.rem(x + nx - j, nx)
            part = home.at[src, :, cols]
            pltpu.make_async_remote_copy(
                src_ref=part, dst_ref=part, send_sem=hs_sem.at[i, j],
                recv_sem=hr_sem.at[i, src], device_id={"node": 2 * src + core},
                device_id_type=MESH,
            ).wait_recv()
        total = jnp.sum(home[:, :, cols].astype(F32), axis=0)
        at = i * quarter
        tg_ref[:, at : at + quarter] = total[:toks, :quarter].astype(BF)
        tg_ref[:, half + at : half + at + quarter] = total[toks:, :quarter].astype(BF)
        return total[:toks, quarter:]

    swap = gather_group(0)
    z_advance(5)
    send_home(0, swap)
    z_advance(6)
    swap = gather_group(1)
    z_advance(7)
    send_home(1, swap)
    home_sum(0)
    z_advance(8)
    weight_dense = home_sum(1)
    slot_lane = lax.broadcasted_iota(jnp.int32, (toks, top), 1)
    weight_out = jnp.zeros((toks, top), F32)
    for k in range(top):
        value = jnp.sum(
            jnp.where(ids[:, k : k + 1] == lane, weight_dense, 0.0), axis=1, keepdims=True
        )
        weight_out = jnp.where(slot_lane == k, value, weight_out)
    wgrad_ref[...] = weight_out.astype(BF)
    for copy in started:
        copy.wait_send()


def body(tokens, cotangent, expert_ids, route_weights, w_gate, w_up, w_down):
    nz, nn, nl = (lax.axis_size(name) for name in ("edata", "node", "local"))
    nx = nn // 2
    toks, width = tokens.shape
    top = expert_ids.shape[1]
    hidden_units = w_gate.shape[2]
    half, quarter, chunk = width // 2, width // 4, hidden_units // nz
    slots, rows = nl * SLOT, nn * SLOT
    vmem = pl.BlockSpec(memory_space=pltpu.VMEM)
    hbm = pl.BlockSpec(memory_space=pltpu.HBM)
    dma = pltpu.SemaphoreType.DMA
    return pl.pallas_call(
        functools.partial(kernel, (nz, nn, nl)),
        out_shape=(
            jax.ShapeDtypeStruct((toks, width), BF),
            jax.ShapeDtypeStruct((toks, top), BF),
            jax.ShapeDtypeStruct((1, chunk, width), F32),
        ),
        in_specs=[hbm] * 7,
        out_specs=(vmem, vmem, vmem),
        scratch_shapes=[
            pltpu.VMEM((toks, width), BF),
            pltpu.VMEM((toks, width), BF),
            pltpu.VMEM((toks, top), jnp.int32),
            pltpu.VMEM((toks, top), BF),
            pltpu.VMEM((width, hidden_units), BF),
            pltpu.VMEM((width, hidden_units), BF),
            pltpu.VMEM((hidden_units, width), BF),
            pltpu.VMEM((nn, SLOT, half + LANES), BF),
            pltpu.VMEM((nn, SLOT, half), BF),
            pltpu.VMEM((2 * slots, rows), BF),
            pltpu.VMEM((rows, 2 * slots), BF),
            pltpu.VMEM((slots, width + LANES), BF),
            pltpu.VMEM((slots, width + LANES), BF),
            pltpu.VMEM((slots, width), BF),
            pltpu.VMEM((slots, width), BF),
            pltpu.VMEM((slots, hidden_units), F32),
            pltpu.VMEM((slots, hidden_units), F32),
            pltpu.VMEM((slots, hidden_units), BF),
            pltpu.VMEM((hidden_units, slots), BF),
            pltpu.VMEM((slots, width), BF),
            pltpu.VMEM((slots, hidden_units), BF),
            pltpu.VMEM((slots, hidden_units), BF),
            pltpu.VMEM((slots, hidden_units), F32),
            pltpu.VMEM((slots, width + LANES), BF),
            pltpu.VMEM((slots, width + LANES), BF),
            pltpu.VMEM((nx, 2, SLOT, half + LANES), BF),
            pltpu.VMEM((nx, SLOT, half + LANES), BF),
            pltpu.VMEM((nx, SLOT, half + LANES), BF),
            pltpu.VMEM((nx, SLOT, half + LANES), BF),
            pltpu.VMEM((hidden_units, width), BF),
            pltpu.VMEM((4, nz - 2, chunk, quarter), BF),
            pltpu.VMEM((4, nz - 1, chunk, quarter), BF),
            dma((7,)),
            dma((3, nx)),
            dma((3, nn)),
            dma((3, nx)),
            dma((10, nl)),
            dma((10, nl)),
            dma((4, nz - 1)),
            dma((4, nz - 1)),
            dma((2, 2)),
            dma((2, nx)),
            dma((2, nx)),
        ],
        compiler_params=pltpu.CompilerParams(
            collective_id=0, has_side_effects=True, vmem_limit_bytes=58 * 1024 * 1024
        ),
        name="expert_layer",
    )(tokens, cotangent, expert_ids, route_weights, w_gate, w_up, w_down)


def solution(mesh):
    in_specs = (
        P(("edata", "node", "local"), None),
        P(("edata", "node", "local"), None),
        P(("edata", "node", "local"), None),
        P(("edata", "node", "local"), None),
        P(("node", "local"), None, None),
        P(("node", "local"), None, None),
        P(("node", "local"), None, None),
    )
    out_specs = (
        P(("edata", "node", "local"), None),
        P(("edata", "node", "local"), None),
        P(("node", "local"), "edata", None),
    )
    return jax.shard_map(body, mesh=mesh, in_specs=in_specs, out_specs=out_specs, check_vma=False)
```

time: 108 us -> 100 us (0.926)
  the two profiles are of different devices: /device:TPU:12 before, /device:TPU:1 now
where the time goes in v2:
time: 100 us; the launch traced here: 98.4 us
  Pallas kernels  93.1 us (93%)
  local copies, waits for them, and re-layouts  4.68 us (5%)
    pallas_call x1, Pallas kernels, body(): pl.pallas_call(functools.partial(kernel, (nz, nn, nl)), out_shape=(jax.Sh...  93.1 us
    unnamed x3, local copies, waits for them, and re-layouts  4.68 us

profile of v2, /device:TPU:1, one launch (start us, length us, event | category | flops | bytes accessed | tf_op | source)
XLA Modules:
  0.0 98.4 jit_solution(11621049449271116223)
XLA Ops:
  0.6 93.1 %expert_layer.1 = (bf16[8,2048]{1,0:T(8,128)(2,1)}, bf16[8,8]{1,0:T(8,128)(2,1)}, f32[1,96,2048]{2,1,0:T(8,128)}) custom-call(bf16[8,2048]{1,0:T(8,128)(2,1)} %tok_hbm.1, bf16[8,2048]{1,0:T(8,128)(2,1)} %cot_hbm.1, s32[8,8]{1,0:T(8,128)} %ids_hbm.1, bf16[8,8]{1,0:T(8,128)(2,1)} %rw_hbm.1, bf16[1,2048,768]{2,1,0:T(8,128)(2,1)} %wg_hbm.1, ...), custom_call_target="tpu_custom_call" | custom-call | tf_op jit(solution)/shard_map/expert_layer/pallas_call | solution.py:417
  93.7 1.4 %copy.13 = bf16[8,2048]{1,0:T(8,128)(2,1)} copy(bf16[8,2048]{1,0:T(8,128)(2,1)} %get-tuple-element.6) | data formatting | bytes 65536
  95.1 1.2 %copy.14 = bf16[8,8]{1,0:T(8,128)(2,1)} copy(bf16[8,8]{1,0:T(8,128)(2,1)} %get-tuple-element.7) | data formatting | bytes 256
  96.3 2.1 %copy.15 = f32[1,96,2048]{2,1,0:T(8,128)} copy(f32[1,96,2048]{2,1,0:T(8,128)} %get-tuple-element.8) | data formatting | bytes 1572864
